TPU v7x, 128 devices: a whole 4x4x4 slice. The times are simulated.
128 devices in a mesh: leaf: 32 (over z, y, x_lo), blk: 4 (over x_hi, core).
Axes of the slice: x: 4 (x_hi: 2, x_lo: 2; x = x_hi * 2 + x_lo), y: 4, z: 4, core: 2. Of those that a mesh axis runs over, the one named last changes fastest.
Arguments:
- noise_root: float32 [4096, 512], P('blk'), may hold values from -6 to 6
- block_root: bfloat16 [4096, 4096], P('leaf', 'blk'), as said below
- noise_first: float32 [2048, 1024], P('blk', 'leaf'), may hold values from -6 to 6
- block_first: bfloat16 [4096, 2048], P('leaf', 'blk'), as said below
- coupling_first: bfloat16 [6144, 2048], P('leaf', 'blk'), may hold values from -0.109375 to 0.109375
- structure_first: int32 [6144], P('leaf'), may hold values from 0 to 4095, as said below
- noise_second: float32 [2048, 2048], P('blk', 'leaf'), may hold values from -6 to 6
- block_second: bfloat16 [8192, 2048], P('leaf', 'blk'), as said below
- coupling_second: bfloat16 [12288, 2048], P('leaf', 'blk'), may hold values from -0.109375 to 0.109375
- structure_second: int32 [12288], P('leaf'), may hold values from 0 to 6143, as said below
- noise_third: float32 [1024, 4096], P('blk', 'leaf'), may hold values from -6 to 6
- block_third: bfloat16 [8192, 1024], P('leaf', 'blk'), as said below
- coupling_third: bfloat16 [24576, 1024], P('leaf', 'blk'), may hold values from -0.109375 to 0.109375
- structure_third: int32 [24576], P('leaf'), may hold values from 0 to 8191, as said below
Outputs:
- solved_root: bfloat16 [4096, 512], P(('leaf', 'blk'))
- solved_first: bfloat16 [4096, 512], P(('leaf', 'blk'))
- solved_second: bfloat16 [8192, 512], P(('leaf', 'blk'))
- solved_third: bfloat16 [8192, 512], P(('leaf', 'blk'))
Inputs may be any that keep to these rules, and one draw needn't show every extreme that they name: `structure_first`: for each first-level supernode, its 3072 entries are distinct, ascending, and include 0 and 4095. `structure_second`: for each second-level supernode, its 3072 entries are distinct, ascending, and include 0 and 6143. `structure_third`: for each third-level supernode, its 3072 entries are distinct, ascending, and include 0 and 8191. `block_root`: tiles above the diagonal tiles are zero; diagonal tiles are lower triangular with positive diagonals. `block_first`: in each supernode's square block, tiles above the diagonal tiles are zero; diagonal tiles are lower triangular with positive diagonals. `block_second`: in each supernode's square block, tiles above the diagonal tiles are zero; diagonal tiles are lower triangular with positive diagonals. `block_third`: in each supernode's square block, tiles above the diagonal tiles are zero; diagonal tiles are lower triangular with positive diagonals.
All inputs are finite; a program needn't handle non-finite values.
Results may differ from a plain program's by a relative error of at most 0.012.
Values may be sent and summed in bfloat16 or wider, within the bound.
No kernel may reach another device: no remote copies, remote signals or barrier semaphores. Data moves between devices by JAX's collectives and lax.ppermute only.
A program may use at most 128 MiB of HBM per device.

v0:
```python
import jax
import jax.numpy as jnp
from jax import lax
from jax.sharding import PartitionSpec as P


def partner(block, axis, bit):
    count = lax.axis_size(axis)
    route = []
    for low in range(count):
        high = low | 1 << bit
        if high != low and high < count:
            route += [(low, high), (high, low)]
    return lax.ppermute(block, axis, route)


def broadcast(array, axis, root):
    mine = lax.axis_index(axis) == root
    return lax.psum(jnp.where(mine, array, jnp.zeros_like(array)), axis)


def transposed_product(left, right):
    return lax.dot_general(
        left, right, (((0,), (0,)), ((), ())), preferred_element_type=jnp.float32
    )


def gather_group(local_rows, group_index, level_bits):
    entire = lax.all_gather(local_rows, "leaf", axis=0, tiled=True)
    span_rows = local_rows.shape[0] << level_bits
    return lax.dynamic_slice_in_dim(entire, group_index * span_rows, span_rows, 0)


def sum_in_group(partial_value, level_bits):
    total = partial_value
    for bit_number in range(level_bits):
        total = total + partner(total, "leaf", bit_number)
    return total


def solve_chain(column_tile, residual, blk_index, blk_count, tile_rows):
    inverse = lax.dynamic_slice_in_dim(column_tile, blk_index * tile_rows, tile_rows, 0)
    accumulated = jnp.zeros(residual.shape, jnp.float32)
    solutions = [None] * blk_count

    def own_solve(right_side):
        return transposed_product(inverse, right_side).astype(jnp.bfloat16)

    def no_solve(right_side):
        return jnp.zeros(right_side.shape, jnp.bfloat16)

    for target in reversed(range(blk_count)):
        right_side = (residual - accumulated).astype(jnp.bfloat16)
        own_tile = lax.cond(blk_index == target, own_solve, no_solve, right_side)
        solved_tile = broadcast(own_tile, "blk", target)
        solutions[target] = solved_tile
        if target > 0:
            tile_block = column_tile[target * tile_rows : (target + 1) * tile_rows]
            contribution = transposed_product(tile_block, solved_tile)
            accumulated = accumulated + jnp.where(blk_index < target, contribution, 0.0)
    return jnp.concatenate(solutions, 0)


def local(
    noise_root,
    block_root,
    noise_first,
    block_first,
    coupling_first,
    structure_first,
    noise_second,
    block_second,
    coupling_second,
    structure_second,
    noise_third,
    block_third,
    coupling_third,
    structure_third,
):
    leaf_index = lax.axis_index("leaf")
    blk_index = lax.axis_index("blk")
    leaf_count = lax.axis_size("leaf")
    blk_count = lax.axis_size("blk")
    levels_data = [
        (noise_root, block_root, None, None),
        (noise_first, block_first, coupling_first, structure_first),
        (noise_second, block_second, coupling_second, structure_second),
        (noise_third, block_third, coupling_third, structure_third),
    ]
    solved = []
    outputs = []
    for level_number, (noise, local_rows, coupling, structure) in enumerate(levels_data):
        group_size = leaf_count >> level_number
        level_bits = group_size.bit_length() - 1
        group_index = leaf_index // group_size
        member_index = leaf_index % group_size
        sep_rows = local_rows.shape[0] * group_size
        tile_rows = local_rows.shape[1]
        column_tile = gather_group(local_rows, group_index, level_bits)
        if level_number == 0:
            residual = noise
        else:
            ancestors = jnp.concatenate(solved, 0)
            picked = jnp.take(ancestors, structure, axis=0)
            partial_value = -transposed_product(coupling, picked)
            columns_each = noise.shape[1]
            noise_full = lax.dynamic_update_slice(
                jnp.zeros(partial_value.shape, jnp.float32), noise, (0, member_index * columns_each)
            )
            residual = sum_in_group(partial_value + noise_full, level_bits)
        supernode = solve_chain(column_tile, residual, blk_index, blk_count, tile_rows)
        solved.append(supernode)
        out_rows = sep_rows // (group_size * blk_count)
        start_row = member_index * (sep_rows // group_size) + blk_index * out_rows
        outputs.append(lax.dynamic_slice_in_dim(supernode, start_row, out_rows, 0))
    return (outputs[0], outputs[1], outputs[2], outputs[3])


def solution(mesh):
    in_specs = (
        P("blk", None),
        P("leaf", "blk"),
        P("blk", "leaf"),
        P("leaf", "blk"),
        P("leaf", "blk"),
        P("leaf"),
        P("blk", "leaf"),
        P("leaf", "blk"),
        P("leaf", "blk"),
        P("leaf"),
        P("blk", "leaf"),
        P("leaf", "blk"),
        P("leaf", "blk"),
        P("leaf"),
    )
    out_specs = (
        P(("leaf", "blk"), None),
        P(("leaf", "blk"), None),
        P(("leaf", "blk"), None),
        P(("leaf", "blk"), None),
    )
    return jax.shard_map(local, mesh=mesh, in_specs=in_specs, out_specs=out_specs, check_vma=False)
```

profile of v0, /device:TPU:1, one launch (start us, length us, event | category | flops | bytes accessed | tf_op | source)
XLA Modules:
  0.0 1534.2 jit_solution(11518332723813780028)
XLA Ops:
  10.7 192.3 %all-gather.5.cloned.1.call-done = bf16[4096,1024]{1,0:T(8,128)(2,1)} async-done(((bf16[128,1024]{1,0:T(8,128)(2,1)}), bf16[4096,1024]{1,0:T(8,128)(2,1)}) %all-gather.5.cloned.1.call-update) | async-done | bytes 8388624 | tf_op jit(solution)/shard_map/all_gather | solution.py:29
  209.9 43.1 %all-reduce.17.cloned.1.call-done = bf16[1024,512]{1,0:T(8,128)(2,1)} async-done(((bf16[1024,512]{1,0:T(8,128)(2,1)}), bf16[1024,512]{1,0:T(8,128)(2,1)}) %all-reduce.17.cloned.1.call-update) | async-done | bytes 1048592 | tf_op jit(solution)/shard_map/psum | solution.py:19
  253.0 5.5 fusion.8
  259.7 48.3 %all-reduce.19.cloned.1.call-done = bf16[1024,512]{1,0:T(8,128)(2,1)} async-done(((bf16[1024,512]{1,0:T(8,128)(2,1)}), bf16[1024,512]{1,0:T(8,128)(2,1)}) %all-reduce.19.cloned.1.call-update) | async-done | bytes 1048592 | tf_op jit(solution)/shard_map/psum | solution.py:19
  308.0 5.5 subtract_convert_fusion
  317.9 44.1 %all-reduce.21.cloned.1.call-done = bf16[1024,512]{1,0:T(8,128)(2,1)} async-done(((bf16[1024,512]{1,0:T(8,128)(2,1)}), bf16[1024,512]{1,0:T(8,128)(2,1)}) %all-reduce.21.cloned.1.call-update) | async-done | bytes 1048592 | tf_op jit(solution)/shard_map/psum | solution.py:19
  367.9 46.1 %all-reduce.23.cloned.1.call-done = bf16[1024,512]{1,0:T(8,128)(2,1)} async-done(((bf16[1024,512]{1,0:T(8,128)(2,1)}), bf16[1024,512]{1,0:T(8,128)(2,1)}) %all-reduce.23.cloned.1.call-update) | async-done | bytes 1048592 | tf_op jit(solution)/shard_map/psum | solution.py:19
  427.6 44.2 %collective-permute-done = f32[512,512]{0,1:T(8,128)S(1)} collective-permute-done((f32[512,512]{0,1:T(8,128)S(1)}, f32[512,512]{0,1:T(8,128)S(1)}, u32[]{:S(2)}, u32[]{:S(2)}) %collective-permute-start) | collective-permute-done | bytes 1048608 | tf_op jit(solution)/shard_map/ppermute | solution.py:14
  472.1 4.2 collective-permute-start.1
  476.3 31.1 %collective-permute-done.1 = f32[512,512]{0,1:T(8,128)S(1)} collective-permute-done((f32[512,512]{0,1:T(8,128)S(1)}, f32[512,512]{0,1:T(8,128)S(1)}, u32[]{:S(2)}, u32[]{:S(2)}) %collective-permute-start.1) | collective-permute-done | bytes 1048608 | tf_op jit(solution)/shard_map/ppermute | solution.py:14
  511.3 33.4 %collective-permute-done.2 = f32[512,512]{0,1:T(8,128)S(1)} collective-permute-done((f32[512,512]{0,1:T(8,128)S(1)}, f32[512,512]{0,1:T(8,128)S(1)}, u32[]{:S(2)}, u32[]{:S(2)}) %collective-permute-start.2) | collective-permute-done | bytes 1048608 | tf_op jit(solution)/shard_map/ppermute | solution.py:14
  547.6 25.0 %all-gather.7.cloned.1.call-done = bf16[4096,512]{1,0:T(8,128)(2,1)} async-done(((bf16[128,512]{1,0:T(8,128)(2,1)}), bf16[4096,512]{1,0:T(8,128)(2,1)}) %all-gather.7.cloned.1.call-update) | async-done | bytes 4194320 | tf_op jit(solution)/shard_map/all_gather | solution.py:29
  576.9 56.2 %all-reduce.25.cloned.1.call-done = bf16[512,512]{1,0:T(8,128)(2,1)} async-done(((bf16[512,512]{1,0:T(8,128)(2,1)}), bf16[512,512]{1,0:T(8,128)(2,1)}) %all-reduce.25.cloned.1.call-update) | async-done | bytes 524304 | tf_op jit(solution)/shard_map/psum | solution.py:19
  636.5 43.0 %all-reduce.27.cloned.1.call-done = bf16[512,512]{1,0:T(8,128)(2,1)} async-done(((bf16[512,512]{1,0:T(8,128)(2,1)}), bf16[512,512]{1,0:T(8,128)(2,1)}) %all-reduce.27.cloned.1.call-update) | async-done | bytes 524304 | tf_op jit(solution)/shard_map/psum | solution.py:19
  683.6 41.2 %all-reduce.29.cloned.1.call-done = bf16[512,512]{1,0:T(8,128)(2,1)} async-done(((bf16[512,512]{1,0:T(8,128)(2,1)}), bf16[512,512]{1,0:T(8,128)(2,1)}) %all-reduce.29.cloned.1.call-update) | async-done | bytes 524304 | tf_op jit(solution)/shard_map/psum | solution.py:19
  729.5 41.8 %all-reduce.31.cloned.1.call-done = bf16[512,512]{1,0:T(8,128)(2,1)} async-done(((bf16[512,512]{1,0:T(8,128)(2,1)}), bf16[512,512]{1,0:T(8,128)(2,1)}) %all-reduce.31.cloned.1.call-update) | async-done | bytes 524304 | tf_op jit(solution)/shard_map/psum | solution.py:19
  776.7 5.7 gather_fusion.1
  783.4 47.2 %collective-permute-done.4 = f32[512,512]{0,1:T(8,128)S(1)} collective-permute-done((f32[512,512]{0,1:T(8,128)S(1)}, f32[512,512]{0,1:T(8,128)S(1)}, u32[]{:S(2)}, u32[]{:S(2)}) %collective-permute-start.4) | collective-permute-done | bytes 1048608 | tf_op jit(solution)/shard_map/ppermute | solution.py:14
  832.1 43.3 %collective-permute-done.5 = f32[512,512]{0,1:T(8,128)S(1)} collective-permute-done((f32[512,512]{0,1:T(8,128)S(1)}, f32[512,512]{0,1:T(8,128)S(1)}, u32[]{:S(2)}, u32[]{:S(2)}) %collective-permute-start.5) | collective-permute-done | bytes 1048608 | tf_op jit(solution)/shard_map/ppermute | solution.py:14
  878.6 102.6 %all-gather.9.cloned.1.call-done = bf16[8192,512]{1,0:T(8,128)(2,1)} async-done(((bf16[256,512]{1,0:T(8,128)(2,1)}), bf16[8192,512]{1,0:T(8,128)(2,1)}) %all-gather.9.cloned.1.call-update) | async-done | bytes 8388624 | tf_op jit(solution)/shard_map/all_gather | solution.py:29
  985.9 46.8 %all-reduce.33.cloned.1.call-done = bf16[512,512]{1,0:T(8,128)(2,1)} async-done(((bf16[512,512]{1,0:T(8,128)(2,1)}), bf16[512,512]{1,0:T(8,128)(2,1)}) %all-reduce.33.cloned.1.call-update) | async-done | bytes 524304 | tf_op jit(solution)/shard_map/psum | solution.py:19
  1037.2 43.1 %all-reduce.35.cloned.1.call-done = bf16[512,512]{1,0:T(8,128)(2,1)} async-done(((bf16[512,512]{1,0:T(8,128)(2,1)}), bf16[512,512]{1,0:T(8,128)(2,1)}) %all-reduce.35.cloned.1.call-update) | async-done | bytes 524304 | tf_op jit(solution)/shard_map/psum | solution.py:19
  1086.6 41.0 %all-reduce.37.cloned.1.call-done = bf16[512,512]{1,0:T(8,128)(2,1)} async-done(((bf16[512,512]{1,0:T(8,128)(2,1)}), bf16[512,512]{1,0:T(8,128)(2,1)}) %all-reduce.37.cloned.1.call-update) | async-done | bytes 524304 | tf_op jit(solution)/shard_map/psum | solution.py:19
  1134.6 41.3 %all-reduce.39.cloned.1.call-done = bf16[512,512]{1,0:T(8,128)(2,1)} async-done(((bf16[512,512]{1,0:T(8,128)(2,1)}), bf16[512,512]{1,0:T(8,128)(2,1)}) %all-reduce.39.cloned.1.call-update) | async-done | bytes 524304 | tf_op jit(solution)/shard_map/psum | solution.py:19
  1180.3 7.2 gather_fusion.2
  1189.6 21.2 %collective-permute-done.7 = f32[256,512]{0,1:T(8,128)S(1)} collective-permute-done((f32[256,512]{0,1:T(8,128)S(1)}, f32[256,512]{0,1:T(8,128)S(1)}, u32[]{:S(2)}, u32[]{:S(2)}) %collective-permute-start.7) | collective-permute-done | bytes 524320 | tf_op jit(solution)/shard_map/ppermute | solution.py:14
  1210.8 4.5 collective-permute-start.8
  1215.3 113.1 %all-gather.11.cloned.1.call-done = bf16[8192,256]{1,0:T(8,128)(2,1)} async-done(((bf16[256,256]{1,0:T(8,128)(2,1)}), bf16[8192,256]{1,0:T(8,128)(2,1)}) %all-gather.11.cloned.1.call-update) | async-done | bytes 4194320 | tf_op jit(solution)/shard_map/all_gather | solution.py:29
  1332.7 56.4 %all-reduce.41.cloned.1.call-done = bf16[256,512]{1,0:T(8,128)(2,1)} async-done(((bf16[256,512]{1,0:T(8,128)(2,1)}), bf16[256,512]{1,0:T(8,128)(2,1)}) %all-reduce.41.cloned.1.call-update) | async-done | bytes 262160 | tf_op jit(solution)/shard_map/psum | solution.py:19
  1392.7 42.2 %all-reduce.43.cloned.1.call-done = bf16[256,512]{1,0:T(8,128)(2,1)} async-done(((bf16[256,512]{1,0:T(8,128)(2,1)}), bf16[256,512]{1,0:T(8,128)(2,1)}) %all-reduce.43.cloned.1.call-update) | async-done | bytes 262160 | tf_op jit(solution)/shard_map/psum | solution.py:19
  1441.0 39.4 %all-reduce.45.cloned.1.call-done = bf16[256,512]{1,0:T(8,128)(2,1)} async-done(((bf16[256,512]{1,0:T(8,128)(2,1)}), bf16[256,512]{1,0:T(8,128)(2,1)}) %all-reduce.45.cloned.1.call-update) | async-done | bytes 262160 | tf_op jit(solution)/shard_map/psum | solution.py:19
  1488.4 37.4 %all-reduce.47.cloned.1.call-done = bf16[256,512]{1,0:T(8,128)(2,1)} async-done(((bf16[256,512]{1,0:T(8,128)(2,1)}), bf16[256,512]{1,0:T(8,128)(2,1)}) %all-reduce.47.cloned.1.call-update) | async-done | bytes 262160 | tf_op jit(solution)/shard_map/psum | solution.py:19
  (203 shorter events, 134.1 us)
Async XLA Ops:
  7.2 775.2 %copy-start = (bf16[384,512]{1,0:T(8,128)(2,1)S(1)}, bf16[384,512]{1,0:T(8,128)(2,1)}, u32[]{:S(2)}) copy-start(bf16[384,512]{1,0:T(8,128)(2,1)} %param.54) | copy-start | bytes 1179652
  7.2 195.8 %all-gather.5.cloned.1.call-start = ((), (), s32[]{:S(2)}) async-start(), calls=%async_computation | async-start | bytes 8650752 | tf_op jit(solution)/shard_map/all_gather | solution.py:29
  7.9 245.1 %all-reduce.17.cloned.1.call-start = ((), (), s32[]{:S(2)}) async-start(), calls=%async_computation.1 | async-start | bytes 2097152 | tf_op jit(solution)/shard_map/psum | solution.py:19
  207.2 100.8 %all-reduce.19.cloned.1.call-start = ((), (), s32[]{:S(2)}) async-start(), calls=%async_computation.2 | async-start | bytes 2097152 | tf_op jit(solution)/shard_map/psum | solution.py:19
  259.6 102.3 %all-reduce.21.cloned.1.call-start = ((), (), s32[]{:S(2)}) async-start(), calls=%async_computation.3 | async-start | bytes 2097152 | tf_op jit(solution)/shard_map/psum | solution.py:19
  317.8 96.1 %all-reduce.23.cloned.1.call-start = ((), (), s32[]{:S(2)}) async-start(), calls=%async_computation.4 | async-start | bytes 2097152 | tf_op jit(solution)/shard_map/psum | solution.py:19
  367.0 205.6 %all-gather.7.cloned.1.call-start = ((), (), s32[]{:S(2)}) async-start(), calls=%async_computation.5 | async-start | bytes 4325376 | tf_op jit(solution)/shard_map/all_gather | solution.py:29
  367.6 265.5 %all-reduce.25.cloned.1.call-start = ((), (), s32[]{:S(2)}) async-start(), calls=%async_computation.6 | async-start | bytes 1048576 | tf_op jit(solution)/shard_map/psum | solution.py:19
  427.3 44.6 %collective-permute-start = (f32[512,512]{0,1:T(8,128)S(1)}, f32[512,512]{0,1:T(8,128)S(1)}, u32[]{:S(2)}, u32[]{:S(2)}) collective-permute-start(f32[512,512]{0,1:T(8,128)S(1)} %fusion.51), channel_id=1, source_target_pairs={{0,4},{4,0},{8,12},{12,8},{16,20},{20,16},{24,28},{28,24},{32,36},... | collective-permute-start | bytes 3145736 | tf_op jit(solution)/shard_map/ppermute | solution.py:14
  472.1 35.3 %collective-permute-start.1 = (f32[512,512]{0,1:T(8,128)S(1)}, f32[512,512]{0,1:T(8,128)S(1)}, u32[]{:S(2)}, u32[]{:S(2)}) collective-permute-start(f32[512,512]{0,1:T(8,128)S(1)} %add.208), channel_id=1, source_target_pairs={{0,8},{8,0},{4,12},{12,4},{16,24},{24,16},{20,28},{28,20},{32,40},... | collective-permute-start | bytes 3145736 | tf_op jit(solution)/shard_map/ppermute | solution.py:14
  507.6 37.1 %collective-permute-start.2 = (f32[512,512]{0,1:T(8,128)S(1)}, f32[512,512]{0,1:T(8,128)S(1)}, u32[]{:S(2)}, u32[]{:S(2)}) collective-permute-start(f32[512,512]{0,1:T(8,128)S(1)} %add.209), channel_id=1, source_target_pairs={{0,16},{16,0},{4,20},{20,4},{8,24},{24,8},{12,28},{28,12},{32,48},... | collective-permute-start | bytes 3145736 | tf_op jit(solution)/shard_map/ppermute | solution.py:14
  544.9 29.6 %collective-permute-start.3 = (f32[512,512]{0,1:T(8,128)S(1)}, f32[512,512]{0,1:T(8,128)}, u32[]{:S(2)}, u32[]{:S(2)}) collective-permute-start(f32[512,512]{0,1:T(8,128)S(1)} %add.210), channel_id=1, source_target_pairs={{0,32},{32,0},{4,36},{36,4},{8,40},{40,8},{12,44},{44,12},{16,48},... | collective-permute-start | bytes 3145736 | tf_op jit(solution)/shard_map/ppermute | solution.py:14
  576.8 102.6 %all-reduce.27.cloned.1.call-start = ((), (), s32[]{:S(2)}) async-start(), calls=%async_computation.7 | async-start | bytes 1048576 | tf_op jit(solution)/shard_map/psum | solution.py:19
  636.5 88.4 %all-reduce.29.cloned.1.call-start = ((), (), s32[]{:S(2)}) async-start(), calls=%async_computation.8 | async-start | bytes 1048576 | tf_op jit(solution)/shard_map/psum | solution.py:19
  683.6 87.7 %all-reduce.31.cloned.1.call-start = ((), (), s32[]{:S(2)}) async-start(), calls=%async_computation.9 | async-start | bytes 1048576 | tf_op jit(solution)/shard_map/psum | solution.py:19
  728.6 252.5 %all-gather.9.cloned.1.call-start = ((), (), s32[]{:S(2)}) async-start(), calls=%async_computation.10 | async-start | bytes 8650752 | tf_op jit(solution)/shard_map/all_gather | solution.py:29
  729.4 303.4 %all-reduce.33.cloned.1.call-start = ((), (), s32[]{:S(2)}) async-start(), calls=%async_computation.11 | async-start | bytes 1048576 | tf_op jit(solution)/shard_map/psum | solution.py:19
  783.1 47.6 %collective-permute-start.4 = (f32[512,512]{0,1:T(8,128)S(1)}, f32[512,512]{0,1:T(8,128)S(1)}, u32[]{:S(2)}, u32[]{:S(2)}) collective-permute-start(f32[512,512]{0,1:T(8,128)S(1)} %fusion.43), channel_id=1, source_target_pairs={{0,4},{4,0},{8,12},{12,8},{16,20},{20,16},{24,28},{28,24},{32,36},... | collective-permute-start | bytes 3145736 | tf_op jit(solution)/shard_map/ppermute | solution.py:14
  830.9 44.6 %collective-permute-start.5 = (f32[512,512]{0,1:T(8,128)S(1)}, f32[512,512]{0,1:T(8,128)S(1)}, u32[]{:S(2)}, u32[]{:S(2)}) collective-permute-start(f32[512,512]{0,1:T(8,128)S(1)} %add.222), channel_id=1, source_target_pairs={{0,8},{8,0},{4,12},{12,4},{16,24},{24,16},{20,28},{28,20},{32,40},... | collective-permute-start | bytes 3145736 | tf_op jit(solution)/shard_map/ppermute | solution.py:14
  875.7 106.7 %copy-start.11 = (f32[512,512]{0,1:T(8,128)}, f32[512,512]{0,1:T(8,128)S(1)}, u32[]{:S(2)}) copy-start(f32[512,512]{0,1:T(8,128)S(1)} %add.223) | copy-start | bytes 3145732
  875.7 106.7 %collective-permute-start.6 = (f32[512,512]{0,1:T(8,128)S(1)}, f32[512,512]{0,1:T(8,128)}, u32[]{:S(2)}, u32[]{:S(2)}) collective-permute-start(f32[512,512]{0,1:T(8,128)S(1)} %add.223), channel_id=1, source_target_pairs={{0,16},{16,0},{4,20},{20,4},{8,24},{24,8},{12,28},{28,12},{32,48},... | collective-permute-start | bytes 3145736 | tf_op jit(solution)/shard_map/ppermute | solution.py:14
  985.9 94.5 %all-reduce.35.cloned.1.call-start = ((), (), s32[]{:S(2)}) async-start(), calls=%async_computation.12 | async-start | bytes 1048576 | tf_op jit(solution)/shard_map/psum | solution.py:19
  1037.2 90.5 %all-reduce.37.cloned.1.call-start = ((), (), s32[]{:S(2)}) async-start(), calls=%async_computation.13 | async-start | bytes 1048576 | tf_op jit(solution)/shard_map/psum | solution.py:19
  1086.6 89.3 %all-reduce.39.cloned.1.call-start = ((), (), s32[]{:S(2)}) async-start(), calls=%async_computation.14 | async-start | bytes 1048576 | tf_op jit(solution)/shard_map/psum | solution.py:19
  1132.2 196.2 %all-gather.11.cloned.1.call-start = ((), (), s32[]{:S(2)}) async-start(), calls=%async_computation.15 | async-start | bytes 4325376 | tf_op jit(solution)/shard_map/all_gather | solution.py:29
  1132.8 256.2 %all-reduce.41.cloned.1.call-start = ((), (), s32[]{:S(2)}) async-start(), calls=%async_computation.16 | async-start | bytes 524288 | tf_op jit(solution)/shard_map/psum | solution.py:19
  1189.2 21.5 %collective-permute-start.7 = (f32[256,512]{0,1:T(8,128)S(1)}, f32[256,512]{0,1:T(8,128)S(1)}, u32[]{:S(2)}, u32[]{:S(2)}) collective-permute-start(f32[256,512]{0,1:T(8,128)S(1)} %fusion.42), channel_id=1, source_target_pairs={{0,4},{4,0},{8,12},{12,8},{16,20},{20,16},{24,28},{28,24},{32,36},... | collective-permute-start | bytes 1572872 | tf_op jit(solution)/shard_map/ppermute | solution.py:14
  1210.8 119.2 %collective-permute-start.8 = (f32[256,512]{0,1:T(8,128)S(1)}, f32[256,512]{0,1:T(8,128)}, u32[]{:S(2)}, u32[]{:S(2)}) collective-permute-start(f32[256,512]{0,1:T(8,128)S(1)} %add.236), channel_id=1, source_target_pairs={{0,8},{8,0},{4,12},{12,4},{16,24},{24,16},{20,28},{28,20},{32,40},... | collective-permute-start | bytes 1572872 | tf_op jit(solution)/shard_map/ppermute | solution.py:14
  1332.6 102.2 %all-reduce.43.cloned.1.call-start = ((), (), s32[]{:S(2)}) async-start(), calls=%async_computation.17 | async-start | bytes 524288 | tf_op jit(solution)/shard_map/psum | solution.py:19
  1391.9 93.6 %copy-start.7 = (bf16[512,512]{1,0:T(8,128)(2,1)S(1)}, bf16[512,512]{1,0:T(8,128)(2,1)}, u32[]{:S(2)}) copy-start(bf16[512,512]{1,0:T(8,128)(2,1)} %all-reduce.29.cloned.1.call-done) | copy-start | bytes 1572868
  1392.6 87.8 %all-reduce.45.cloned.1.call-start = ((), (), s32[]{:S(2)}) async-start(), calls=%async_computation.18 | async-start | bytes 524288 | tf_op jit(solution)/shard_map/psum | solution.py:19
  1440.9 84.9 %all-reduce.47.cloned.1.call-start = ((), (), s32[]{:S(2)}) async-start(), calls=%async_computation.19 | async-start | bytes 524288 | tf_op jit(solution)/shard_map/psum | solution.py:19
  (19 other events, 578.8 us)
Sparse Core Ops, SparseCore 0:
  9.7 193.2 all-gather.4
  207.3 45.6 all-reduce.16
  259.8 48.2 all-reduce.18
  317.9 44.0 all-reduce.20
  367.1 46.7 all-reduce.22
  415.4 157.1 all-gather.6
  576.9 56.0 all-reduce.24
  636.6 42.8 all-reduce.26
  683.7 41.0 all-reduce.28
  728.8 42.4 all-reduce.30
  772.9 208.1 all-gather.8
  986.0 46.7 all-reduce.32
  1037.3 42.9 all-reduce.34
  1086.7 40.8 all-reduce.36
  1132.3 43.4 all-reduce.38
  1177.4 150.9 all-gather.10
  1332.7 56.2 all-reduce.40
  1392.7 42.0 all-reduce.42
  1441.0 39.3 all-reduce.44
  1484.2 41.5 all-reduce.46
where the time goes:
time: 1540 us; the launch traced here: 1530 us
  waiting for transfers between devices  1370 us (89%)
  local copies, waits for them, and re-layouts  53.6 us (3%)
  matrix products  46.8 us (3%)
  other arithmetic  29.5 us (2%)
  starting transfers between devices  21.4 us (1%)
    psum x16, waiting for transfers between devices, broadcast(): return lax.psum(jnp.where(mine, array, jnp.zeros_like(array)), axis)  711 us
    all_gather x4, waiting for transfers between devices, gather_group(): entire = lax.all_gather(local_rows, 'leaf', axis=0, tiled=True)  433 us
    ppermute x9, waiting for transfers between devices, partner(): return lax.ppermute(block, axis, route)  221 us
    dot_general x19, matrix products, transposed_product(): lax.dot_general(left, right, (((0,), (0,)), ((), ())), preferred_element_...  46.8 us
  transfers between devices with their start and end apart: 29, of which 27 were waited for; matrix products, arithmetic and copies ran while one was open for 4% of the time, Pallas kernels for 0%

commit v1 on v0

--- a/solution.py
+++ b/solution.py
@@ -26,7 +26,9 @@
 
 
 def gather_group(local_rows, group_index, level_bits):
-    entire = lax.all_gather(local_rows, "leaf", axis=0, tiled=True)
+    entire = jnp.concatenate(
+        lax.all_to_all(jnp.stack([local_rows] * lax.axis_size("leaf")), "leaf", 0, 0), axis=0
+    )
     span_rows = local_rows.shape[0] << level_bits
     return lax.dynamic_slice_in_dim(entire, group_index * span_rows, span_rows, 0)
 

time: 1540 us -> 1310 us (0.85)
  waiting for transfers between devices: 1370 us -> 1090 us
  starting transfers between devices: 21.4 us -> 45.1 us
  local copies, waits for them, and re-layouts: 53.6 us -> 76.1 us
    all_gather x4 -> x0, waiting for transfers between devices: 433 us -> none  [gather_group(): entire = lax.all_gather(local_rows, 'leaf', axis=0, tiled=True)]
    all_to_all x0 -> x4, waiting for transfers between devices: none -> 123 us  [gather_group(): lax.all_to_all(jnp.stack([local_rows] * lax.axis_size('leaf')), 'leaf', 0...]
    all_to_all x0 -> x4, starting transfers between devices: none -> 32.3 us  [gather_group(): lax.all_to_all(jnp.stack([local_rows] * lax.axis_size('leaf')), 'leaf', 0...]
    psum x16, waiting for transfers between devices: 711 us -> 736 us  [broadcast(): return lax.psum(jnp.where(mine, array, jnp.zeros_like(array)), axis)]
    another operation x12 -> x16, local copies, waits for them, and re-layouts: 5.14 us -> 20.8 us  [the longest x4 15.6 us: gather_group(): jnp.stack([local_rows] * lax.axis_size('leaf'))]
  transfers between devices with their start and end apart: 29 -> 29, of which waited for: 27 -> 26; matrix products, arithmetic and copies ran while one was open for 4% -> 6% of each run, Pallas kernels for 0% -> 0%
where the time goes in v1:
time: 1310 us; the launch traced here: 1300 us
  waiting for transfers between devices  1090 us (83%)
  local copies, waits for them, and re-layouts  76.1 us (6%)
  starting transfers between devices  45.1 us (3%)
  matrix products  44.3 us (3%)
  other arithmetic  26.1 us (2%)
  between operations  14.9 us (1%)
    psum x16, waiting for transfers between devices, broadcast(): return lax.psum(jnp.where(mine, array, jnp.zeros_like(array)), axis)  736 us
    ppermute x9, waiting for transfers between devices, partner(): return lax.ppermute(block, axis, route)  234 us
    all_to_all x4, waiting for transfers between devices, gather_group(): lax.all_to_all(jnp.stack([local_rows] * lax.axis_size('leaf')), 'leaf', 0...  123 us
    dot_general x19, matrix products, transposed_product(): lax.dot_general(left, right, (((0,), (0,)), ((), ())), preferred_element_...  44.3 us
    all_to_all x4, starting transfers between devices, gather_group(): lax.all_to_all(jnp.stack([local_rows] * lax.axis_size('leaf')), 'leaf', 0...  32.3 us
  transfers between devices with their start and end apart: 29, of which 26 were waited for; matrix products, arithmetic and copies ran while one was open for 6% of the time, Pallas kernels for 0%

profile of v1, /device:TPU:1, one launch (start us, length us, event | category | flops | bytes accessed | tf_op | source)
XLA Modules:
  0.0 1299.6 jit_solution(11637760116140924355)
XLA Ops:
  12.6 10.1 all-to-all-start
  22.9 122.7 %all-to-all-done = bf16[32,128,1024]{2,1,0:T(8,128)(2,1)} async-done(((bf16[32,128,1024]{2,1,0:T(8,128)(2,1)}), bf16[32,128,1024]{2,1,0:T(8,128)(2,1)}, u32[]{:S(2)}, u32[]{:S(2)}) %all-to-all-start) | async-done | bytes 8388640 | tf_op jit(solution)/shard_map/all_to_all | solution.py:30
  151.8 5.7 fusion.60
  157.6 53.8 %all-reduce.17.cloned.1.call-done = bf16[1024,512]{1,0:T(8,128)(2,1)} async-done(((bf16[1024,512]{1,0:T(8,128)(2,1)}), bf16[1024,512]{1,0:T(8,128)(2,1)}) %all-reduce.17.cloned.1.call-update) | async-done | bytes 1048592 | tf_op jit(solution)/shard_map/psum | solution.py:19
  217.5 48.4 %all-reduce.19.cloned.1.call-done = bf16[1024,512]{1,0:T(8,128)(2,1)} async-done(((bf16[1024,512]{1,0:T(8,128)(2,1)}), bf16[1024,512]{1,0:T(8,128)(2,1)}) %all-reduce.19.cloned.1.call-update) | async-done | bytes 1048592 | tf_op jit(solution)/shard_map/psum | solution.py:19
  275.6 44.1 %all-reduce.21.cloned.1.call-done = bf16[1024,512]{1,0:T(8,128)(2,1)} async-done(((bf16[1024,512]{1,0:T(8,128)(2,1)}), bf16[1024,512]{1,0:T(8,128)(2,1)}) %all-reduce.21.cloned.1.call-update) | async-done | bytes 1048592 | tf_op jit(solution)/shard_map/psum | solution.py:19
  325.3 46.9 %all-reduce.23.cloned.1.call-done = bf16[1024,512]{1,0:T(8,128)(2,1)} async-done(((bf16[1024,512]{1,0:T(8,128)(2,1)}), bf16[1024,512]{1,0:T(8,128)(2,1)}) %all-reduce.23.cloned.1.call-update) | async-done | bytes 1048592 | tf_op jit(solution)/shard_map/psum | solution.py:19
  390.2 8.0 all-to-all-start.1
  398.2 13.9 %collective-permute-done = f32[512,512]{0,1:T(8,128)S(1)} collective-permute-done((f32[512,512]{0,1:T(8,128)S(1)}, f32[512,512]{0,1:T(8,128)S(1)}, u32[]{:S(2)}, u32[]{:S(2)}) %collective-permute-start) | collective-permute-done | bytes 1048608 | tf_op jit(solution)/shard_map/ppermute | solution.py:14
  413.6 60.4 %collective-permute-done.1 = f32[512,512]{0,1:T(8,128)S(1)} collective-permute-done((f32[512,512]{0,1:T(8,128)S(1)}, f32[512,512]{0,1:T(8,128)S(1)}, u32[]{:S(2)}, u32[]{:S(2)}) %collective-permute-start.1) | collective-permute-done | bytes 1048608 | tf_op jit(solution)/shard_map/ppermute | solution.py:14
  476.7 22.2 %collective-permute-done.2 = f32[512,512]{0,1:T(8,128)S(1)} collective-permute-done((f32[512,512]{0,1:T(8,128)S(1)}, f32[512,512]{0,1:T(8,128)S(1)}, u32[]{:S(2)}, u32[]{:S(2)}) %collective-permute-start.2) | collective-permute-done | bytes 1048608 | tf_op jit(solution)/shard_map/ppermute | solution.py:14
  504.8 7.1 all-to-all-start.2
  513.1 47.4 %collective-permute-done.3 = f32[512,512]{0,1:T(8,128)} collective-permute-done((f32[512,512]{0,1:T(8,128)S(1)}, f32[512,512]{0,1:T(8,128)}, u32[]{:S(2)}, u32[]{:S(2)}) %collective-permute-start.3) | collective-permute-done | bytes 1048608 | tf_op jit(solution)/shard_map/ppermute | solution.py:14
  563.0 89.2 %all-reduce.25.cloned.1.call-done = bf16[512,512]{1,0:T(8,128)(2,1)} async-done(((bf16[512,512]{1,0:T(8,128)(2,1)}), bf16[512,512]{1,0:T(8,128)(2,1)}) %all-reduce.25.cloned.1.call-update) | async-done | bytes 524304 | tf_op jit(solution)/shard_map/psum | solution.py:19
  655.6 43.1 %all-reduce.27.cloned.1.call-done = bf16[512,512]{1,0:T(8,128)(2,1)} async-done(((bf16[512,512]{1,0:T(8,128)(2,1)}), bf16[512,512]{1,0:T(8,128)(2,1)}) %all-reduce.27.cloned.1.call-update) | async-done | bytes 524304 | tf_op jit(solution)/shard_map/psum | solution.py:19
  702.9 41.2 %all-reduce.29.cloned.1.call-done = bf16[512,512]{1,0:T(8,128)(2,1)} async-done(((bf16[512,512]{1,0:T(8,128)(2,1)}), bf16[512,512]{1,0:T(8,128)(2,1)}) %all-reduce.29.cloned.1.call-update) | async-done | bytes 524304 | tf_op jit(solution)/shard_map/psum | solution.py:19
  748.2 42.4 %all-reduce.31.cloned.1.call-done = bf16[512,512]{1,0:T(8,128)(2,1)} async-done(((bf16[512,512]{1,0:T(8,128)(2,1)}), bf16[512,512]{1,0:T(8,128)(2,1)}) %all-reduce.31.cloned.1.call-update) | async-done | bytes 524304 | tf_op jit(solution)/shard_map/psum | solution.py:19
  802.5 24.3 %collective-permute-done.4 = f32[512,512]{0,1:T(8,128)S(1)} collective-permute-done((f32[512,512]{0,1:T(8,128)S(1)}, f32[512,512]{0,1:T(8,128)S(1)}, u32[]{:S(2)}, u32[]{:S(2)}) %collective-permute-start.4) | collective-permute-done | bytes 1048608 | tf_op jit(solution)/shard_map/ppermute | solution.py:14
  828.4 22.5 %collective-permute-done.5 = f32[512,512]{0,1:T(8,128)S(1)} collective-permute-done((f32[512,512]{0,1:T(8,128)S(1)}, f32[512,512]{0,1:T(8,128)S(1)}, u32[]{:S(2)}, u32[]{:S(2)}) %collective-permute-start.5) | collective-permute-done | bytes 1048608 | tf_op jit(solution)/shard_map/ppermute | solution.py:14
  855.0 20.5 %collective-permute-done.6 = f32[512,512]{0,1:T(8,128)} collective-permute-done((f32[512,512]{0,1:T(8,128)S(1)}, f32[512,512]{0,1:T(8,128)}, u32[]{:S(2)}, u32[]{:S(2)}) %collective-permute-start.6) | collective-permute-done | bytes 1048608 | tf_op jit(solution)/shard_map/ppermute | solution.py:14
  879.1 44.3 %all-reduce.33.cloned.1.call-done = bf16[512,512]{1,0:T(8,128)(2,1)} async-done(((bf16[512,512]{1,0:T(8,128)(2,1)}), bf16[512,512]{1,0:T(8,128)(2,1)}) %all-reduce.33.cloned.1.call-update) | async-done | bytes 524304 | tf_op jit(solution)/shard_map/psum | solution.py:19
  931.3 7.1 all-to-all-start.3
  938.4 36.5 %all-reduce.35.cloned.1.call-done = bf16[512,512]{1,0:T(8,128)(2,1)} async-done(((bf16[512,512]{1,0:T(8,128)(2,1)}), bf16[512,512]{1,0:T(8,128)(2,1)}) %all-reduce.35.cloned.1.call-update) | async-done | bytes 524304 | tf_op jit(solution)/shard_map/psum | solution.py:19
  982.9 41.6 %all-reduce.37.cloned.1.call-done = bf16[512,512]{1,0:T(8,128)(2,1)} async-done(((bf16[512,512]{1,0:T(8,128)(2,1)}), bf16[512,512]{1,0:T(8,128)(2,1)}) %all-reduce.37.cloned.1.call-update) | async-done | bytes 524304 | tf_op jit(solution)/shard_map/psum | solution.py:19
  1029.3 43.6 %all-reduce.39.cloned.1.call-done = bf16[512,512]{1,0:T(8,128)(2,1)} async-done(((bf16[512,512]{1,0:T(8,128)(2,1)}), bf16[512,512]{1,0:T(8,128)(2,1)}) %all-reduce.39.cloned.1.call-update) | async-done | bytes 524304 | tf_op jit(solution)/shard_map/psum | solution.py:19
  1077.3 7.2 gather_fusion.2
  1085.6 13.1 %collective-permute-done.7 = f32[256,512]{0,1:T(8,128)S(1)} collective-permute-done((f32[256,512]{0,1:T(8,128)S(1)}, f32[256,512]{0,1:T(8,128)S(1)}, u32[]{:S(2)}, u32[]{:S(2)}) %collective-permute-start.7) | collective-permute-done | bytes 524320 | tf_op jit(solution)/shard_map/ppermute | solution.py:14
  1101.8 9.8 collective-permute-done.8
  1113.6 41.8 %all-reduce.41.cloned.1.call-done = bf16[256,512]{1,0:T(8,128)(2,1)} async-done(((bf16[256,512]{1,0:T(8,128)(2,1)}), bf16[256,512]{1,0:T(8,128)(2,1)}) %all-reduce.41.cloned.1.call-update) | async-done | bytes 262160 | tf_op jit(solution)/shard_map/psum | solution.py:19
  1158.2 42.2 %all-reduce.43.cloned.1.call-done = bf16[256,512]{1,0:T(8,128)(2,1)} async-done(((bf16[256,512]{1,0:T(8,128)(2,1)}), bf16[256,512]{1,0:T(8,128)(2,1)}) %all-reduce.43.cloned.1.call-update) | async-done | bytes 262160 | tf_op jit(solution)/shard_map/psum | solution.py:19
  1206.5 39.4 %all-reduce.45.cloned.1.call-done = bf16[256,512]{1,0:T(8,128)(2,1)} async-done(((bf16[256,512]{1,0:T(8,128)(2,1)}), bf16[256,512]{1,0:T(8,128)(2,1)}) %all-reduce.45.cloned.1.call-update) | async-done | bytes 262160 | tf_op jit(solution)/shard_map/psum | solution.py:19
  1253.9 37.4 %all-reduce.47.cloned.1.call-done = bf16[256,512]{1,0:T(8,128)(2,1)} async-done(((bf16[256,512]{1,0:T(8,128)(2,1)}), bf16[256,512]{1,0:T(8,128)(2,1)}) %all-reduce.47.cloned.1.call-update) | async-done | bytes 262160 | tf_op jit(solution)/shard_map/psum | solution.py:19
  (214 shorter events, 159.4 us)
Async XLA Ops:
  7.2 794.3 %copy-start = (bf16[384,512]{1,0:T(8,128)(2,1)S(1)}, bf16[384,512]{1,0:T(8,128)(2,1)}, u32[]{:S(2)}) copy-start(bf16[384,512]{1,0:T(8,128)(2,1)} %param.54) | copy-start | bytes 1179652
  12.6 133.0 %all-to-all-start = ((bf16[32,128,1024]{2,1,0:T(8,128)(2,1)}), bf16[32,128,1024]{2,1,0:T(8,128)(2,1)}, u32[]{:S(2)}, u32[]{:S(2)}) async-start(bf16[32,128,1024]{2,1,0:T(8,128)(2,1)} %stack.8), calls=%async_computation | async-start | bytes 16777216 | tf_op jit(solution)/shard_map/all_to_all | solution.py:30
  22.6 188.8 %all-reduce.17.cloned.1.call-start = ((), (), s32[]{:S(2)}) async-start(), calls=%async_computation.4 | async-start | bytes 2097152 | tf_op jit(solution)/shard_map/psum | solution.py:19
  149.8 116.0 %all-reduce.19.cloned.1.call-start = ((), (), s32[]{:S(2)}) async-start(), calls=%async_computation.5 | async-start | bytes 2097152 | tf_op jit(solution)/shard_map/psum | solution.py:19
  217.4 102.4 %all-reduce.21.cloned.1.call-start = ((), (), s32[]{:S(2)}) async-start(), calls=%async_computation.6 | async-start | bytes 2097152 | tf_op jit(solution)/shard_map/psum | solution.py:19
  275.6 96.6 %all-reduce.23.cloned.1.call-start = ((), (), s32[]{:S(2)}) async-start(), calls=%async_computation.7 | async-start | bytes 2097152 | tf_op jit(solution)/shard_map/psum | solution.py:19
  387.3 24.8 %collective-permute-start = (f32[512,512]{0,1:T(8,128)S(1)}, f32[512,512]{0,1:T(8,128)S(1)}, u32[]{:S(2)}, u32[]{:S(2)}) collective-permute-start(f32[512,512]{0,1:T(8,128)S(1)} %fusion.41), channel_id=1, source_target_pairs={{0,4},{4,0},{8,12},{12,8},{16,20},{20,16},{24,28},{28,24},{32,36},... | collective-permute-start | bytes 3145736 | tf_op jit(solution)/shard_map/ppermute | solution.py:14
  390.2 110.4 %all-to-all-start.1 = ((bf16[32,128,512]{2,1,0:T(8,128)(2,1)}), bf16[32,128,512]{2,1,0:T(8,128)(2,1)}, u32[]{:S(2)}, u32[]{:S(2)}) async-start(bf16[32,128,512]{2,1,0:T(8,128)(2,1)} %stack.9), calls=%async_computation.1 | async-start | bytes 8388608 | tf_op jit(solution)/shard_map/all_to_all | solution.py:30
  398.2 102.3 %copy-start.18 = (bf16[256,512]{1,0:T(8,128)(2,1)S(1)}, bf16[256,512]{1,0:T(8,128)(2,1)}, u32[]{:S(2)}) copy-start(bf16[256,512]{1,0:T(8,128)(2,1)} %param.53) | copy-start | bytes 786436
  412.3 61.6 %collective-permute-start.1 = (f32[512,512]{0,1:T(8,128)S(1)}, f32[512,512]{0,1:T(8,128)S(1)}, u32[]{:S(2)}, u32[]{:S(2)}) collective-permute-start(f32[512,512]{0,1:T(8,128)S(1)} %add.208), channel_id=1, source_target_pairs={{0,8},{8,0},{4,12},{12,4},{16,24},{24,16},{20,28},{28,20},{32,40},... | collective-permute-start | bytes 3145736 | tf_op jit(solution)/shard_map/ppermute | solution.py:14
  474.2 24.7 %collective-permute-start.2 = (f32[512,512]{0,1:T(8,128)S(1)}, f32[512,512]{0,1:T(8,128)S(1)}, u32[]{:S(2)}, u32[]{:S(2)}) collective-permute-start(f32[512,512]{0,1:T(8,128)S(1)} %add.209), channel_id=1, source_target_pairs={{0,16},{16,0},{4,20},{20,4},{8,24},{24,8},{12,28},{28,12},{32,48},... | collective-permute-start | bytes 3145736 | tf_op jit(solution)/shard_map/ppermute | solution.py:14
  499.1 61.5 %collective-permute-start.3 = (f32[512,512]{0,1:T(8,128)S(1)}, f32[512,512]{0,1:T(8,128)}, u32[]{:S(2)}, u32[]{:S(2)}) collective-permute-start(f32[512,512]{0,1:T(8,128)S(1)} %add.210), channel_id=1, source_target_pairs={{0,32},{32,0},{4,36},{36,4},{8,40},{40,8},{12,44},{44,12},{16,48},... | collective-permute-start | bytes 3145736 | tf_op jit(solution)/shard_map/ppermute | solution.py:14
  504.8 349.1 %all-to-all-start.2 = ((bf16[32,256,512]{2,1,0:T(8,128)(2,1)}), bf16[32,256,512]{2,1,0:T(8,128)(2,1)}, u32[]{:S(2)}, u32[]{:S(2)}) async-start(bf16[32,256,512]{2,1,0:T(8,128)(2,1)} %stack.10), calls=%async_computation.2 | async-start | bytes 16777216 | tf_op jit(solution)/shard_map/all_to_all | solution.py:30
  511.9 140.2 %all-reduce.25.cloned.1.call-start = ((), (), s32[]{:S(2)}) async-start(), calls=%async_computation.8 | async-start | bytes 1048576 | tf_op jit(solution)/shard_map/psum | solution.py:19
  562.9 135.8 %all-reduce.27.cloned.1.call-start = ((), (), s32[]{:S(2)}) async-start(), calls=%async_computation.9 | async-start | bytes 1048576 | tf_op jit(solution)/shard_map/psum | solution.py:19
  655.6 88.5 %all-reduce.29.cloned.1.call-start = ((), (), s32[]{:S(2)}) async-start(), calls=%async_computation.10 | async-start | bytes 1048576 | tf_op jit(solution)/shard_map/psum | solution.py:19
  702.8 87.7 %all-reduce.31.cloned.1.call-start = ((), (), s32[]{:S(2)}) async-start(), calls=%async_computation.11 | async-start | bytes 1048576 | tf_op jit(solution)/shard_map/psum | solution.py:19
  747.9 175.5 %all-reduce.33.cloned.1.call-start = ((), (), s32[]{:S(2)}) async-start(), calls=%async_computation.12 | async-start | bytes 1048576 | tf_op jit(solution)/shard_map/psum | solution.py:19
  802.2 24.7 %collective-permute-start.4 = (f32[512,512]{0,1:T(8,128)S(1)}, f32[512,512]{0,1:T(8,128)S(1)}, u32[]{:S(2)}, u32[]{:S(2)}) collective-permute-start(f32[512,512]{0,1:T(8,128)S(1)} %fusion.33), channel_id=1, source_target_pairs={{0,4},{4,0},{8,12},{12,8},{16,20},{20,16},{24,28},{28,24},{32,36},... | collective-permute-start | bytes 3145736 | tf_op jit(solution)/shard_map/ppermute | solution.py:14
  827.1 23.8 %collective-permute-start.5 = (f32[512,512]{0,1:T(8,128)S(1)}, f32[512,512]{0,1:T(8,128)S(1)}, u32[]{:S(2)}, u32[]{:S(2)}) collective-permute-start(f32[512,512]{0,1:T(8,128)S(1)} %add.222), channel_id=1, source_target_pairs={{0,8},{8,0},{4,12},{12,4},{16,24},{24,16},{20,28},{28,20},{32,40},... | collective-permute-start | bytes 3145736 | tf_op jit(solution)/shard_map/ppermute | solution.py:14
  851.0 24.4 %collective-permute-start.6 = (f32[512,512]{0,1:T(8,128)S(1)}, f32[512,512]{0,1:T(8,128)}, u32[]{:S(2)}, u32[]{:S(2)}) collective-permute-start(f32[512,512]{0,1:T(8,128)S(1)} %add.223), channel_id=1, source_target_pairs={{0,16},{16,0},{4,20},{20,4},{8,24},{24,8},{12,28},{28,12},{32,48},... | collective-permute-start | bytes 3145736 | tf_op jit(solution)/shard_map/ppermute | solution.py:14
  879.1 95.9 %all-reduce.35.cloned.1.call-start = ((), (), s32[]{:S(2)}) async-start(), calls=%async_computation.13 | async-start | bytes 1048576 | tf_op jit(solution)/shard_map/psum | solution.py:19
  931.3 169.0 %all-to-all-start.3 = ((bf16[32,256,256]{2,1,0:T(8,128)(2,1)}), bf16[32,256,256]{2,1,0:T(8,128)(2,1)}, u32[]{:S(2)}, u32[]{:S(2)}) async-start(bf16[32,256,256]{2,1,0:T(8,128)(2,1)} %stack.11), calls=%async_computation.3 | async-start | bytes 8388608 | tf_op jit(solution)/shard_map/all_to_all | solution.py:30
  938.4 86.2 %all-reduce.37.cloned.1.call-start = ((), (), s32[]{:S(2)}) async-start(), calls=%async_computation.14 | async-start | bytes 1048576 | tf_op jit(solution)/shard_map/psum | solution.py:19
  981.2 91.6 %all-reduce.39.cloned.1.call-start = ((), (), s32[]{:S(2)}) async-start(), calls=%async_computation.15 | async-start | bytes 1048576 | tf_op jit(solution)/shard_map/psum | solution.py:19
  1029.2 126.2 %all-reduce.41.cloned.1.call-start = ((), (), s32[]{:S(2)}) async-start(), calls=%async_computation.16 | async-start | bytes 524288 | tf_op jit(solution)/shard_map/psum | solution.py:19
  1085.2 13.4 %collective-permute-start.7 = (f32[256,512]{0,1:T(8,128)S(1)}, f32[256,512]{0,1:T(8,128)S(1)}, u32[]{:S(2)}, u32[]{:S(2)}) collective-permute-start(f32[256,512]{0,1:T(8,128)S(1)} %fusion.32), channel_id=1, source_target_pairs={{0,4},{4,0},{8,12},{12,8},{16,20},{20,16},{24,28},{28,24},{32,36},... | collective-permute-start | bytes 1572872 | tf_op jit(solution)/shard_map/ppermute | solution.py:14
  1098.8 12.8 collective-permute-start.8
  1113.5 86.9 %all-reduce.43.cloned.1.call-start = ((), (), s32[]{:S(2)}) async-start(), calls=%async_computation.17 | async-start | bytes 524288 | tf_op jit(solution)/shard_map/psum | solution.py:19
  1157.4 93.5 %copy-start.7 = (bf16[512,512]{1,0:T(8,128)(2,1)S(1)}, bf16[512,512]{1,0:T(8,128)(2,1)}, u32[]{:S(2)}) copy-start(bf16[512,512]{1,0:T(8,128)(2,1)} %all-reduce.29.cloned.1.call-done) | copy-start | bytes 1572868
  1158.2 87.7 %all-reduce.45.cloned.1.call-start = ((), (), s32[]{:S(2)}) async-start(), calls=%async_computation.18 | async-start | bytes 524288 | tf_op jit(solution)/shard_map/psum | solution.py:19
  1206.4 84.9 %all-reduce.47.cloned.1.call-start = ((), (), s32[]{:S(2)}) async-start(), calls=%async_computation.19 | async-start | bytes 524288 | tf_op jit(solution)/shard_map/psum | solution.py:19
  (24 other events, 616.8 us)
Sparse Core Ops, SparseCore 0:
  150.0 61.4 all-reduce.16
  217.5 48.2 all-reduce.18
  275.7 44.0 all-reduce.20
  325.4 46.7 all-reduce.22
  563.1 89.0 all-reduce.24
  655.7 42.9 all-reduce.26
  702.9 41.0 all-reduce.28
  748.0 42.4 all-reduce.30
  879.2 44.1 all-reduce.32
  927.9 47.0 all-reduce.34
  981.3 43.1 all-reduce.36
  1029.3 43.4 all-reduce.38
  1113.7 41.6 all-reduce.40
  1158.3 42.0 all-reduce.42
  1206.5 39.3 all-reduce.44
  1249.6 41.5 all-reduce.46
